TPU v7x, 32 devices: a whole 2x2x4 slice. The times are simulated.
32 devices in a mesh: dp: 4 (over z), expert: 4 (over y, core), tensor: 2 (over x).
Axes of the slice: x: 2, y: 2, z: 4, core: 2. Of those that a mesh axis runs over, the one named last changes fastest.
Arguments:
- tokens: bfloat16 [1024, 3072], P('expert', 'dp'), may hold values from -6 to 6
- route_ids: int32 [1024, 2], P('expert'), may hold values from 0 to 3, all different within a row; in each aligned block of 256 rows (0 to 255, 256 to 511, ...) at most 128 rows name the same one
- gates: float32 [1024, 2], P('expert'), may hold values from 0.2 to 1
- w_gate: bfloat16 [4, 3072, 8192], P('expert', 'dp', 'tensor'), may hold values from -0.109375 to 0.109375
- w_up: bfloat16 [4, 3072, 8192], P('expert', 'dp', 'tensor'), may hold values from -0.109375 to 0.109375
- w_down: bfloat16 [4, 8192, 3072], P('expert', 'tensor', 'dp'), may hold values from -0.0625 to 0.0625
Outputs:
- mixed: bfloat16 [1024, 3072], P('expert', 'dp')
Inputs may be any that keep to these rules, and one draw needn't show every extreme that they name: `route_ids`: each token names two different experts. Among the 256 tokens of one index of expert, no expert is named by more than 128 tokens, a bound that some block reaches.
All inputs are finite; a program needn't handle non-finite values.
Results may differ from a plain program's by a relative error of at most 0.025.
Values may be sent and summed in bfloat16 or wider, within the bound.
No kernel may reach another device: no remote copies, remote signals or barrier semaphores. Data moves between devices by JAX's collectives and lax.ppermute only.
A program may use at most 64 MiB of HBM per device.

v0:
```python
import jax
import jax.numpy as jnp
from jax import lax
from jax.sharding import PartitionSpec as P


def slot_index(route_group, experts):
    flat = route_group.reshape(-1)
    hits = (flat[:, None] == jnp.arange(experts, dtype=jnp.int32)[None, :]).astype(jnp.int32)
    before = jnp.cumsum(hits, axis=0) - hits
    rank = jnp.sum(before * hits, axis=1)
    return (rank * experts + flat).reshape(-1, 2)


def activate(summed, hidden_units):
    return (jax.nn.silu(summed[..., :hidden_units]) * summed[..., hidden_units:]).astype(
        jnp.bfloat16
    )


def local(tokens, route_ids, gates, w_gate, w_up, w_down):
    experts = lax.axis_size("expert")
    tensor_devices = lax.axis_size("tensor")
    tok_rows = tokens.shape[0]
    width = tokens.shape[1]
    hidden_units = w_gate.shape[2]
    capacity = max(3 * tok_rows // 8, 2 * tok_rows // experts)
    capacity = (capacity + 15) // 16 * 16
    share_slots = capacity // tensor_devices
    places = slot_index(route_ids, experts)
    lines = 0 * experts + jnp.arange(capacity * experts, dtype=jnp.int32)
    chosen = (lines[:, None] == places[None, :, 0]) | (lines[:, None] == places[None, :, 1])
    picked = jnp.dot(chosen.astype(jnp.bfloat16), tokens, preferred_element_type=jnp.float32)
    received = lax.all_to_all(
        picked.astype(jnp.bfloat16).reshape(capacity, experts, width),
        "expert",
        split_axis=1,
        concat_axis=1,
        tiled=True,
    )
    rows = received.reshape(capacity * experts, width)
    gate_part = jnp.dot(rows, w_gate[0], preferred_element_type=jnp.float32).astype(jnp.bfloat16)
    up_part = jnp.dot(rows, w_up[0], preferred_element_type=jnp.float32).astype(jnp.bfloat16)
    both = jnp.concatenate([gate_part, up_part], axis=1)
    summed = lax.psum_scatter(
        both.reshape(capacity, experts, 2 * hidden_units), "dp", scatter_dimension=0, tiled=True
    ).astype(jnp.float32)
    hidden = lax.all_gather(activate(summed, hidden_units), "dp", axis=0, tiled=True)
    piece = hidden.reshape(share_slots * lax.axis_size("tensor") * experts, hidden_units)
    result = jnp.dot(piece, w_down[0], preferred_element_type=jnp.float32)
    finished = lax.psum_scatter(
        result.reshape(share_slots * lax.axis_size("tensor"), experts, width).astype(jnp.bfloat16),
        "tensor",
        scatter_dimension=0,
        tiled=True,
    )
    complete = lax.all_gather(finished, "tensor", axis=0, tiled=True)
    returned = lax.all_to_all(complete, "expert", split_axis=1, concat_axis=1, tiled=True)
    table = returned.reshape(capacity * experts, width)
    first_rows = table[places[:, 0]].astype(jnp.float32)
    second_rows = table[places[:, 1]].astype(jnp.float32)
    mixed = gates[:, 0:1] * first_rows + gates[:, 1:2] * second_rows
    return mixed.astype(jnp.bfloat16)


def solution(mesh):
    return jax.shard_map(
        local,
        mesh=mesh,
        in_specs=(
            P("expert", "dp"),
            P("expert", None),
            P("expert", None),
            P("expert", "dp", "tensor"),
            P("expert", "dp", "tensor"),
            P("expert", "tensor", "dp"),
        ),
        out_specs=P("expert", "dp"),
        check_vma=False,
    )
```

profile of v0, /device:TPU:0, one launch (start us, length us, event | category | flops | bytes accessed | tf_op | source)
XLA Modules:
  0.0 367.2 jit_solution(1575154677809169609)
XLA Ops:
  6.5 0.0 copy-start
  6.5 0.0 reduce-scatter.3.cloned.1.call-start
  6.5 0.9 copy.24
  7.4 0.1 eq.60
  7.6 0.1 eq.56
  7.7 1.2 reduce-window.6
  8.9 0.2 slice_reduce_fusion.2
  9.1 0.2 reduce-window.9
  9.3 0.1 add_bitcast_fusion
  9.4 0.1 mul.45
  9.6 0.3 fusion.20
  9.9 0.0 copy-done
  9.9 0.4 convolution_convert_fusion
  10.3 0.2 reshape.41
  10.5 0.1 copy.27
  10.6 15.7 %all_to_all.10 = bf16[128,4,768]{2,0,1:T(8,128)(2,1)S(1)} all-to-all(bf16[128,4,768]{2,0,1:T(8,128)(2,1)S(1)} %copy.27), channel_id=1, replica_groups=mesh['dp'=4,'expert'=4,'tensor'=2] {'expert'}, dimensions={1} | all-to-all | bytes 1572864 | tf_op jit(solution)/shard_map/all_to_all | solution.py:34
  26.3 0.6 copy.28
  26.9 0.2 reshape.42
  27.1 7.7 %fusion.6 = bf16[512,4096]{1,0:T(8,128)(2,1)} fusion(bf16[512,768]{1,0:T(8,128)(2,1)S(1)} %reshape.42, bf16[1,768,4096]{2,1,0:T(8,128)(2,1)} %param.9), kind=kOutput, calls=%fused_computation.9 | convolution fusion | flops 3223322624 | bytes 11272192 | tf_op jit(solution)/shard_map/dot_general | solution.py:42
  34.8 7.7 %fusion.9 = bf16[512,4096]{1,0:T(8,128)(2,1)} fusion(bf16[512,768]{1,0:T(8,128)(2,1)S(1)} %reshape.42, bf16[1,768,4096]{2,1,0:T(8,128)(2,1)} %param.10), kind=kOutput, calls=%fused_computation.10 | convolution fusion | flops 3223322624 | bytes 11272192 | tf_op jit(solution)/shard_map/dot_general | solution.py:43
  42.5 7.7 %pad_maximum_fusion = bf16[512,8192]{1,0:T(8,128)(2,1)} fusion(bf16[512,4096]{1,0:T(8,128)(2,1)} %fusion.9, bf16[512,4096]{1,0:T(8,128)(2,1)} %fusion.6), kind=kLoop, calls=%fused_computation.2 | loop fusion | flops 16777216 | bytes 16777216 | tf_op jit(solution)/shard_map/concatenate | solution.py:44
  50.2 13.1 %reshape.43 = bf16[128,4,8192]{2,1,0:T(4,128)(2,1)} reshape(bf16[512,8192]{1,0:T(8,128)(2,1)} %pad_maximum_fusion) | data formatting | bytes 16777216 | tf_op jit(solution)/shard_map/reshape | solution.py:46
  63.2 11.2 %copy.29 = bf16[128,4,8192]{2,0,1:T(8,128)(2,1)} copy(bf16[128,4,8192]{2,1,0:T(4,128)(2,1)} %reshape.43) | data formatting | bytes 16777216 | tf_op jit(solution)/shard_map/reshape | solution.py:46
  74.4 0.0 reduce-scatter.3.cloned.1.call-update
  74.5 0.2 all-gather.2.cloned.1.call-start
  74.7 144.7 %reduce-scatter.3.cloned.1.call-done = bf16[32,4,8192]{2,0,1:T(8,128)(2,1)} async-done(((bf16[128,4,8192]{2,0,1:T(8,128)(2,1)}), bf16[32,4,8192]{2,0,1:T(8,128)(2,1)}) %reduce-scatter.3.cloned.1.call-update) | async-done | bytes 2097168 | tf_op jit(solution)/shard_map/reduce_scatter | solution.py:45
  219.4 2.0 convert_element_type.40
  221.4 1.6 fusion.12
  223.0 0.0 all-gather.2.cloned.1.call-update
  223.0 0.0 copy-start.2
  223.0 0.0 reduce-scatter.5.cloned.1.call-start
  223.1 81.6 %all-gather.2.cloned.1.call-done = bf16[128,4,4096]{2,0,1:T(8,128)(2,1)} async-done(((bf16[32,4,4096]{2,0,1:T(8,128)(2,1)}), bf16[128,4,4096]{2,0,1:T(8,128)(2,1)}) %all-gather.2.cloned.1.call-update) | async-done | bytes 4194320 | tf_op jit(solution)/shard_map/all_gather | solution.py:48
  304.6 8.3 %fusion.13 = bf16[128,4,768]{2,0,1:T(8,128)(2,1)} fusion(bf16[128,4,4096]{2,0,1:T(8,128)(2,1)} %all-gather.2.cloned.1.call-done, bf16[1,4096,768]{2,1,0:T(8,128)(2,1)} %param.11), kind=kOutput, calls=%fused_computation.13 | convolution fusion | flops 3221618688 | bytes 11272192 | tf_op jit(solution)/shard_map/dot_general | solution.py:50
  313.0 0.0 reduce-scatter.5.cloned.1.call-update
  313.0 16.1 %reduce-scatter.5.cloned.1.call-done = bf16[64,4,768]{2,0,1:T(8,128)(2,1)} async-done(((bf16[128,4,768]{2,0,1:T(8,128)(2,1)}), bf16[64,4,768]{2,0,1:T(8,128)(2,1)}) %reduce-scatter.5.cloned.1.call-update) | async-done | bytes 393232 | tf_op jit(solution)/shard_map/reduce_scatter | solution.py:51
  329.1 12.2 %all_gather.7 = bf16[128,4,768]{2,0,1:T(8,128)(2,1)} all-gather(bf16[64,4,768]{2,0,1:T(8,128)(2,1)} %reduce-scatter.5.cloned.1.call-done), channel_id=1, replica_groups=mesh['dp'=4,'expert'=4,'tensor'=2] {'tensor'}, dimensions={0}, use_global_device_ids=true | all-gather | bytes 1179648 | tf_op jit(solution)/shard_map/all_gather | solution.py:57
  341.4 3.5 all-to-all-start.1
  344.9 0.0 copy-done.2
  344.9 11.6 %all-to-all-done.1 = bf16[128,4,768]{2,0,1:T(8,128)(2,1)S(1)} async-done(((bf16[128,4,768]{2,0,1:T(8,128)(2,1)}), bf16[128,4,768]{2,0,1:T(8,128)(2,1)S(1)}, u32[]{:S(2)}, u32[]{:S(2)}) %all-to-all-start.1) | async-done | bytes 786464 | tf_op jit(solution)/shard_map/all_to_all | solution.py:58
  356.5 0.6 copy.30
  357.1 0.0 copy-start.1
  357.1 0.2 reshape.44
  357.3 1.2 gather_fusion
  358.5 1.2 gather_fusion.1
  359.7 1.0 add_convert_fusion
  360.6 0.0 copy-done.1
  (6 shorter events, 0.1 us)
Async XLA Ops:
  6.5 3.4 copy-start
  6.5 212.9 %reduce-scatter.3.cloned.1.call-start = ((), (), s32[]{:S(2)}) async-start(), calls=%async_computation.4 | async-start | bytes 10485760 | tf_op jit(solution)/shard_map/reduce_scatter | solution.py:45
  74.5 230.1 %all-gather.2.cloned.1.call-start = ((), (), s32[]{:S(2)}) async-start(), calls=%async_computation.5 | async-start | bytes 5242880 | tf_op jit(solution)/shard_map/all_gather | solution.py:48
  223.0 121.9 %copy-start.2 = (f32[256,2]{0,1:T(2,128)S(1)}, f32[256,2]{0,1:T(2,128)}, u32[]{:S(2)}) copy-start(f32[256,2]{0,1:T(2,128)} %param.8) | copy-start | bytes 6148
  223.0 106.1 %reduce-scatter.5.cloned.1.call-start = ((), (), s32[]{:S(2)}) async-start(), calls=%async_computation.6 | async-start | bytes 1179648 | tf_op jit(solution)/shard_map/reduce_scatter | solution.py:51
  341.4 15.1 %all-to-all-start.1 = ((bf16[128,4,768]{2,0,1:T(8,128)(2,1)}), bf16[128,4,768]{2,0,1:T(8,128)(2,1)S(1)}, u32[]{:S(2)}, u32[]{:S(2)}) async-start(bf16[128,4,768]{2,0,1:T(8,128)(2,1)} %all_gather.7), calls=%async_computation.3 | async-start | bytes 1572864 | tf_op jit(solution)/shard_map/all_to_all | solution.py:58
  357.1 3.5 copy-start.1
Sparse Core Ops, SparseCore 0:
  74.6 144.7 reduce-scatter.2
  223.1 81.4 all-gather.1
  313.1 15.9 reduce-scatter.4
where the time goes:
time: 368 us; the launch traced here: 367 us
  waiting for transfers between devices  254 us (69%)
  local copies, waits for them, and re-layouts  30 us (8%)
  blocking collectives  27.9 us (8%)
  matrix products  24.2 us (7%)
  other arithmetic  14 us (4%)
  between operations  13.3 us (4%)
  starting transfers between devices  3.76 us (1%)
    reduce_scatter x1, waiting for transfers between devices, local(): lax.psum_scatter(both.reshape(capacity, experts, 2 * hidden_units), 'dp',...  145 us
    all_gather x1, waiting for transfers between devices, local(): lax.all_gather(activate(summed, hidden_units), 'dp', axis=0, tiled=True)  81.6 us
    reshape x2, local copies, waits for them, and re-layouts, local(): both.reshape(capacity, experts, 2 * hidden_units)  24.3 us
    reduce_scatter x1, waiting for transfers between devices, local(): lax.psum_scatter(result.reshape(share_slots * lax.axis_size('tensor'), ex...  16.1 us
    all_to_all x1, blocking collectives, local(): lax.all_to_all(picked.astype(jnp.bfloat16).reshape(capacity, experts, wid...  15.7 us
    all_gather x1, blocking collectives, local(): complete = lax.all_gather(finished, 'tensor', axis=0, tiled=True)  12.2 us
    all_to_all x1, waiting for transfers between devices, local(): lax.all_to_all(complete, 'expert', split_axis=1, concat_axis=1, tiled=True)  11.6 us
    dot_general x1, matrix products, local(): result = jnp.dot(piece, w_down[0], preferred_element_type=jnp.float32)  8.35 us
  transfers between devices with their start and end apart: 4, of which 4 were waited for; matrix products, arithmetic and copies ran while one was open for 0% of the time, Pallas kernels for 0%

commit v1 on v0

v1 whole, which is shorter than its diff:
```python
import jax
import jax.numpy as jnp
from jax import lax
from jax.sharding import PartitionSpec as P

F32, BF16 = jnp.float32, jnp.bfloat16


def places_of(ids, experts):
    hits = ids[:, :, None] == jnp.arange(experts, dtype=jnp.int32)
    named = jnp.sum(hits.astype(F32), axis=1).astype(BF16)
    n = ids.shape[0]
    earlier = (jnp.arange(n)[:, None] > jnp.arange(n)[None, :]).astype(BF16)
    before = jnp.dot(earlier, named, preferred_element_type=F32)
    rank = jnp.sum(jnp.where(hits, before[:, None, :], 0.0), axis=2).astype(jnp.int32)
    again = (ids[:, 0] == ids[:, 1]).astype(jnp.int32)
    rank = rank + jnp.stack([jnp.zeros_like(again), again], axis=1)
    return rank * experts + ids


def local(tokens, route_ids, gates, w_gate, w_up, w_down):
    experts = lax.axis_size("expert")
    tensors = lax.axis_size("tensor")
    e = lax.axis_index("expert")
    n, width = tokens.shape
    units = w_gate.shape[2]
    capacity = max(3 * n // 8, 2 * n // experts)
    capacity = (capacity + 15) // 16 * 16
    places = places_of(route_ids, experts)
    rows = []
    for j in range(experts):
        lines = jnp.arange(capacity, dtype=jnp.int32) * experts + (e ^ j)
        chosen = (lines[:, None] == places[None, :, 0]) | (lines[:, None] == places[None, :, 1])
        picked = jnp.dot(chosen.astype(BF16), tokens, preferred_element_type=F32).astype(BF16)
        if j:
            picked = lax.ppermute(picked, "expert", [(a, a ^ j) for a in range(experts)])
        rows.append(picked)

    wg, wu, wd = w_gate[0], w_up[0], w_down[0]
    yields = [jnp.zeros((n, width), F32), jnp.zeros((n, width), F32)]
    for j in range(experts):
        g = jnp.dot(rows[j], wg, preferred_element_type=F32).astype(BF16)
        u = jnp.dot(rows[j], wu, preferred_element_type=F32).astype(BF16)
        both = jnp.concatenate([g, u], axis=1)
        both = lax.psum_scatter(both, "dp", scatter_dimension=0, tiled=True).astype(F32)
        h = (jax.nn.silu(both[:, :units]) * both[:, units:]).astype(BF16)
        h = lax.all_gather(h, "dp", axis=0, tiled=True)
        part = jnp.dot(h, wd, preferred_element_type=F32).astype(BF16)
        if tensors == 2:
            other = lax.ppermute(part, "tensor", [(0, 1), (1, 0)])
            part = (part.astype(F32) + other.astype(F32)).astype(BF16)
        else:
            part = lax.psum(part, "tensor")
        if j:
            part = lax.ppermute(part, "expert", [(a, a ^ j) for a in range(experts)])
        label = jnp.arange(capacity, dtype=jnp.int32) * experts + (e ^ j)
        for k in range(2):
            chosen = (places[:, k : k + 1] == label[None, :]).astype(BF16)
            yields[k] += jnp.dot(chosen, part, preferred_element_type=F32)
    mixed = gates[:, 0:1] * yields[0] + gates[:, 1:2] * yields[1]
    return mixed.astype(BF16)


def solution(mesh):
    return jax.shard_map(
        local,
        mesh=mesh,
        in_specs=(
            P("expert", "dp"),
            P("expert", None),
            P("expert", None),
            P("expert", "dp", "tensor"),
            P("expert", "dp", "tensor"),
            P("expert", "tensor", "dp"),
        ),
        out_specs=P("expert", "dp"),
        check_vma=False,
    )
```

time: 368 us -> 343 us (0.932)
  local copies, waits for them, and re-layouts: 30 us -> 0.32 us
  blocking collectives: 27.9 us -> 0 us
  matrix products: 24.2 us -> 49.4 us
  starting transfers between devices: 3.76 us -> 12.9 us
  waiting for transfers between devices: 254 us -> 249 us
    reduce_scatter x2 -> x4, waiting for transfers between devices: 161 us -> 131 us  [local(): lax.psum_scatter(both, 'dp', scatter_dimension=0, tiled=True).astype(F32)]
    dot_general x4 -> x25, matrix products: 24.2 us -> 49.4 us  [the longest x4 16.4 us: local(): part = jnp.dot(h, wd, preferred_element_type=F32).astype(BF16)]
    reshape x6 -> x0, local copies, waits for them, and re-layouts: 24.9 us -> none  [the longest x2 24.3 us: local(): both.reshape(capacity, experts, 2 * hidden_units)]
    ppermute x0 -> x10, waiting for transfers between devices: none -> 21 us  [the longest x3 11.7 us: local(): lax.ppermute(picked, 'expert', [(a, a ^ j) for a in range(experts)])]
    all_to_all x1 -> x0, blocking collectives: 15.7 us -> none  [local(): lax.all_to_all(picked.astype(jnp.bfloat16).reshape(capacity, experts, wid...]
    all_gather x1 -> x4, waiting for transfers between devices: 81.6 us -> 96.7 us  [local(): h = lax.all_gather(h, 'dp', axis=0, tiled=True)]
    ppermute x0 -> x10, starting transfers between devices: none -> 12.5 us  [the longest x4 6.14 us: local(): other = lax.ppermute(part, 'tensor', [(0, 1), (1, 0)])]
    all_gather x1 -> x0, blocking collectives: 12.2 us -> none  [local(): complete = lax.all_gather(finished, 'tensor', axis=0, tiled=True)]
  transfers between devices with their start and end apart: 4 -> 18, of which waited for: 4 -> 14; matrix products, arithmetic and copies ran while one was open for 0% -> 16% of each run, Pallas kernels for 0% -> 0%
where the time goes in v1:
time: 343 us
  waiting for transfers between devices  249 us (73%)
  matrix products  49.4 us (14%)
  other arithmetic  17 us (5%)
  between operations  13.8 us (4%)
  starting transfers between devices  12.9 us (4%)
    reduce_scatter x4, waiting for transfers between devices, local(): lax.psum_scatter(both, 'dp', scatter_dimension=0, tiled=True).astype(F32)  131 us
    all_gather x4, waiting for transfers between devices, local(): h = lax.all_gather(h, 'dp', axis=0, tiled=True)  96.7 us
    dot_general x4, matrix products, local(): part = jnp.dot(h, wd, preferred_element_type=F32).astype(BF16)  16.4 us
    dot_general x4, matrix products, local(): g = jnp.dot(rows[j], wg, preferred_element_type=F32).astype(BF16)  15.9 us
    dot_general x4, matrix products, local(): u = jnp.dot(rows[j], wu, preferred_element_type=F32).astype(BF16)  12.6 us
    ppermute x3, waiting for transfers between devices, local(): lax.ppermute(picked, 'expert', [(a, a ^ j) for a in range(experts)])  11.7 us
  transfers between devices with their start and end apart: 18, of which 14 were waited for; matrix products, arithmetic and copies ran while one was open for 16% of the time, Pallas kernels for 0%

profile of v1, /device:TPU:0, one launch (start us, length us, event | category | flops | bytes accessed | tf_op | source)
XLA Modules:
  0.0 342.6 jit_solution(2844025407316661211)
XLA Ops:
  6.5 0.7 convert_reduce_fusion
  7.3 0.8 slice_compare_fusion
  8.1 0.2 fusion.72
  8.2 0.7 select_reduce_fusion
  8.9 0.7 fusion.129
  9.7 0.2 convolution_convert_fusion.3
  9.9 4.0 %fusion.24 = bf16[128,4096]{1,0:T(8,128)(2,1)S(1)} fusion(bf16[128,768]{1,0:T(8,128)(2,1)S(1)} %convolution_convert_fusion.3, bf16[1,768,4096]{2,1,0:T(8,128)(2,1)} %param.9), kind=kOutput, calls=%fused_computation.24 | convolution fusion | flops 805830656 | bytes 7536640 | tf_op jit(solution)/shard_map/dot_general | solution.py:42
  13.9 0.3 copy-done.1
  14.2 1.0 fusion.36
  15.2 1.5 pad_maximum_fusion
  16.8 0.2 convolution_convert_fusion.1
  17.1 3.0 collective-permute-start.4
  20.1 4.9 %collective-permute-done.4 = bf16[128,768]{1,0:T(8,128)(2,1)S(1)} collective-permute-done((bf16[128,768]{1,0:T(8,128)(2,1)S(1)}, bf16[128,768]{1,0:T(8,128)(2,1)S(1)}, u32[]{:S(2)}, u32[]{:S(2)}) %collective-permute-start.4) | collective-permute-done | bytes 196640 | tf_op jit(solution)/shard_map/ppermute | solution.py:36
  25.0 4.1 %fusion.30 = bf16[128,4096]{1,0:T(8,128)(2,1)S(1)} fusion(bf16[128,768]{1,0:T(8,128)(2,1)S(1)} %collective-permute-done.4, bf16[1,768,4096]{2,1,0:T(8,128)(2,1)} %param.9), kind=kOutput, calls=%fused_computation.26 | convolution fusion | flops 805830656 | bytes 7536640 | tf_op jit(solution)/shard_map/dot_general | solution.py:42
  29.1 3.9 %fusion.42 = bf16[128,4096]{1,0:T(8,128)(2,1)S(1)} fusion(bf16[128,768]{1,0:T(8,128)(2,1)S(1)} %collective-permute-done.4, bf16[1,768,4096]{2,1,0:T(8,128)(2,1)} %param.10), kind=kOutput, calls=%fused_computation.30 | convolution fusion | flops 805830656 | bytes 7536640 | tf_op jit(solution)/shard_map/dot_general | solution.py:43
  33.0 1.5 pad_maximum_fusion.2
  34.6 0.2 convolution_convert_fusion.2
  34.9 1.4 collective-permute-done.1
  36.4 3.9 %fusion.27 = bf16[128,4096]{1,0:T(8,128)(2,1)S(1)} fusion(bf16[128,768]{1,0:T(8,128)(2,1)S(1)} %collective-permute-done.1, bf16[1,768,4096]{2,1,0:T(8,128)(2,1)} %param.9), kind=kOutput, calls=%fused_computation.25 | convolution fusion | flops 805830656 | bytes 7536640 | tf_op jit(solution)/shard_map/dot_general | solution.py:42
  40.3 3.9 %fusion.39 = bf16[128,4096]{1,0:T(8,128)(2,1)S(1)} fusion(bf16[128,768]{1,0:T(8,128)(2,1)S(1)} %collective-permute-done.1, bf16[1,768,4096]{2,1,0:T(8,128)(2,1)} %param.10), kind=kOutput, calls=%fused_computation.29 | convolution fusion | flops 805830656 | bytes 7536640 | tf_op jit(solution)/shard_map/dot_general | solution.py:43
  44.2 1.5 pad_maximum_fusion.1
  45.7 0.2 convolution_convert_fusion
  46.0 1.6 collective-permute-start.7
  47.6 5.4 %collective-permute-done.7 = bf16[128,768]{1,0:T(8,128)(2,1)S(1)} collective-permute-done((bf16[128,768]{1,0:T(8,128)(2,1)S(1)}, bf16[128,768]{1,0:T(8,128)(2,1)S(1)}, u32[]{:S(2)}, u32[]{:S(2)}) %collective-permute-start.7) | collective-permute-done | bytes 196640 | tf_op jit(solution)/shard_map/ppermute | solution.py:36
  52.9 3.9 %fusion.33 = bf16[128,4096]{1,0:T(8,128)(2,1)S(1)} fusion(bf16[128,768]{1,0:T(8,128)(2,1)S(1)} %collective-permute-done.7, bf16[1,768,4096]{2,1,0:T(8,128)(2,1)} %param.9), kind=kOutput, calls=%fused_computation.27 | convolution fusion | flops 805830656 | bytes 7536640 | tf_op jit(solution)/shard_map/dot_general | solution.py:42
  56.8 3.9 %fusion.45 = bf16[128,4096]{1,0:T(8,128)(2,1)S(1)} fusion(bf16[128,768]{1,0:T(8,128)(2,1)S(1)} %collective-permute-done.7, bf16[1,768,4096]{2,1,0:T(8,128)(2,1)} %param.10), kind=kOutput, calls=%fused_computation.31 | convolution fusion | flops 805830656 | bytes 7536640 | tf_op jit(solution)/shard_map/dot_general | solution.py:43
  60.8 1.5 pad_maximum_fusion.3
  62.3 1.2 reduce-scatter.5.cloned.1.call-done
  63.5 1.1 convert_element_type.141
  64.6 0.8 fusion.71
  65.5 43.6 %reduce-scatter.9.cloned.1.call-done = bf16[32,8192]{1,0:T(8,128)(2,1)} async-done(((bf16[128,8192]{1,0:T(8,128)(2,1)}), bf16[32,8192]{1,0:T(8,128)(2,1)}) %reduce-scatter.9.cloned.1.call-update) | async-done | bytes 524304 | tf_op jit(solution)/shard_map/reduce_scatter | solution.py:45
  109.1 1.1 convert_element_type.159
  110.2 0.8 fusion.69
  111.1 43.5 %reduce-scatter.7.cloned.1.call-done = bf16[32,8192]{1,0:T(8,128)(2,1)} async-done(((bf16[128,8192]{1,0:T(8,128)(2,1)}), bf16[32,8192]{1,0:T(8,128)(2,1)}) %reduce-scatter.7.cloned.1.call-update) | async-done | bytes 524304 | tf_op jit(solution)/shard_map/reduce_scatter | solution.py:45
  154.6 1.1 convert_element_type.150
  155.7 0.9 fusion.70
  156.7 0.2 all-gather.11.cloned.1.call-start
  156.9 43.2 %reduce-scatter.11.cloned.1.call-done = bf16[32,8192]{1,0:T(8,128)(2,1)} async-done(((bf16[128,8192]{1,0:T(8,128)(2,1)}), bf16[32,8192]{1,0:T(8,128)(2,1)}) %reduce-scatter.11.cloned.1.call-update) | async-done | bytes 524304 | tf_op jit(solution)/shard_map/reduce_scatter | solution.py:45
  200.1 1.1 convert_element_type.168
  201.2 0.8 fusion.68
  202.1 26.7 %all-gather.5.cloned.1.call-done = bf16[128,4096]{1,0:T(8,128)(2,1)} async-done(((bf16[32,4096]{1,0:T(8,128)(2,1)}), bf16[128,4096]{1,0:T(8,128)(2,1)}) %all-gather.5.cloned.1.call-update) | async-done | bytes 1048592 | tf_op jit(solution)/shard_map/all_gather | solution.py:47
  228.8 4.1 %fusion.56 = bf16[128,768]{1,0:T(8,128)(2,1)S(1)} fusion(bf16[128,4096]{1,0:T(8,128)(2,1)} %all-gather.5.cloned.1.call-done, bf16[1,4096,768]{2,1,0:T(8,128)(2,1)} %param.11), kind=kOutput, calls=%fused_computation.46 | convolution fusion | flops 805404672 | bytes 7536640 | tf_op jit(solution)/shard_map/dot_general | solution.py:48
  232.9 1.5 collective-permute-start
  234.5 23.2 %all-gather.9.cloned.1.call-done = bf16[128,4096]{1,0:T(8,128)(2,1)} async-done(((bf16[32,4096]{1,0:T(8,128)(2,1)}), bf16[128,4096]{1,0:T(8,128)(2,1)}) %all-gather.9.cloned.1.call-update) | async-done | bytes 1048592 | tf_op jit(solution)/shard_map/all_gather | solution.py:47
  257.7 4.1 %fusion.62 = bf16[128,768]{1,0:T(8,128)(2,1)S(1)} fusion(bf16[128,4096]{1,0:T(8,128)(2,1)} %all-gather.9.cloned.1.call-done, bf16[1,4096,768]{2,1,0:T(8,128)(2,1)} %param.11), kind=kOutput, calls=%fused_computation.48 | convolution fusion | flops 805404672 | bytes 7536640 | tf_op jit(solution)/shard_map/dot_general | solution.py:48
  261.8 1.5 collective-permute-start.5
  263.3 23.4 %all-gather.7.cloned.1.call-done = bf16[128,4096]{1,0:T(8,128)(2,1)} async-done(((bf16[32,4096]{1,0:T(8,128)(2,1)}), bf16[128,4096]{1,0:T(8,128)(2,1)}) %all-gather.7.cloned.1.call-update) | async-done | bytes 1048592 | tf_op jit(solution)/shard_map/all_gather | solution.py:47
  286.7 4.1 %fusion.59 = bf16[128,768]{1,0:T(8,128)(2,1)S(1)} fusion(bf16[128,4096]{1,0:T(8,128)(2,1)} %all-gather.7.cloned.1.call-done, bf16[1,4096,768]{2,1,0:T(8,128)(2,1)} %param.11), kind=kOutput, calls=%fused_computation.47 | convolution fusion | flops 805404672 | bytes 7536640 | tf_op jit(solution)/shard_map/dot_general | solution.py:48
  290.8 1.5 collective-permute-start.2
  292.4 23.4 %all-gather.11.cloned.1.call-done = bf16[128,4096]{1,0:T(8,128)(2,1)} async-done(((bf16[32,4096]{1,0:T(8,128)(2,1)}), bf16[128,4096]{1,0:T(8,128)(2,1)}) %all-gather.11.cloned.1.call-update) | async-done | bytes 1048592 | tf_op jit(solution)/shard_map/all_gather | solution.py:47
  315.8 4.1 %fusion.65 = bf16[128,768]{1,0:T(8,128)(2,1)S(1)} fusion(bf16[128,4096]{1,0:T(8,128)(2,1)} %all-gather.11.cloned.1.call-done, bf16[1,4096,768]{2,1,0:T(8,128)(2,1)} %param.11), kind=kOutput, calls=%fused_computation.49 | convolution fusion | flops 805404672 | bytes 7536640 | tf_op jit(solution)/shard_map/dot_general | solution.py:48
  319.9 1.5 collective-permute-start.8
  321.5 1.5 collective-permute-start.6
  323.1 3.3 collective-permute-done.8
  326.6 1.2 collective-permute-done.6
  327.7 0.3 fusion.75
  328.0 0.3 fusion.88
  328.4 0.3 fusion.77
  328.7 0.3 fusion.93
  329.0 4.8 %collective-permute-done.9 = bf16[128,768]{1,0:T(8,128)(2,1)S(1)} collective-permute-done((bf16[128,768]{1,0:T(8,128)(2,1)S(1)}, bf16[128,768]{1,0:T(8,128)(2,1)S(1)}, u32[]{:S(2)}, u32[]{:S(2)}) %collective-permute-start.9) | collective-permute-done | bytes 196640 | tf_op jit(solution)/shard_map/ppermute | solution.py:55
  333.7 0.3 fusion.73
  334.0 0.3 fusion.83
  334.4 0.3 fusion.50
  334.7 1.1 fusion.55
  (36 shorter events, 0.8 us)
Async XLA Ops:
  6.5 3.1 copy-start
  6.5 57.0 %reduce-scatter.5.cloned.1.call-start = ((), (), s32[]{:S(2)}) async-start(), calls=%async_computation.4 | async-start | bytes 2621440 | tf_op jit(solution)/shard_map/reduce_scatter | solution.py:45
  9.6 4.6 %copy-start.1 = (bf16[1,768,4096]{2,1,0:T(8,128)(2,1)S(1)}, bf16[1,768,4096]{2,1,0:T(8,128)(2,1)}, u32[]{:S(2)}) copy-start(bf16[1,768,4096]{2,1,0:T(8,128)(2,1)} %param.10) | copy-start | bytes 18874372
  16.8 92.3 %reduce-scatter.9.cloned.1.call-start = ((), (), s32[]{:S(2)}) async-start(), calls=%async_computation.8 | async-start | bytes 2621440 | tf_op jit(solution)/shard_map/reduce_scatter | solution.py:45
  17.1 7.9 %collective-permute-start.4 = (bf16[128,768]{1,0:T(8,128)(2,1)S(1)}, bf16[128,768]{1,0:T(8,128)(2,1)S(1)}, u32[]{:S(2)}, u32[]{:S(2)}) collective-permute-start(bf16[128,768]{1,0:T(8,128)(2,1)S(1)} %convolution_convert_fusion.1), channel_id=1, source_target_pairs={{0,4},{2,6},{4,0},{6,2},{1,5},{3,7},{5,1},{7,3},{8,12},{10,14},{12... | collective-permute-start | bytes 589832 | tf_op jit(solution)/shard_map/ppermute | solution.py:36
  34.5 120.1 %reduce-scatter.7.cloned.1.call-start = ((), (), s32[]{:S(2)}) async-start(), calls=%async_computation.6 | async-start | bytes 2621440 | tf_op jit(solution)/shard_map/reduce_scatter | solution.py:45
  34.9 1.5 collective-permute-start.1
  45.7 154.4 %reduce-scatter.11.cloned.1.call-start = ((), (), s32[]{:S(2)}) async-start(), calls=%async_computation.10 | async-start | bytes 2621440 | tf_op jit(solution)/shard_map/reduce_scatter | solution.py:45
  46.0 6.9 %collective-permute-start.7 = (bf16[128,768]{1,0:T(8,128)(2,1)S(1)}, bf16[128,768]{1,0:T(8,128)(2,1)S(1)}, u32[]{:S(2)}, u32[]{:S(2)}) collective-permute-start(bf16[128,768]{1,0:T(8,128)(2,1)S(1)} %convolution_convert_fusion), channel_id=1, source_target_pairs={{0,6},{2,4},{4,2},{6,0},{1,7},{3,5},{5,3},{7,1},{8,14},{10,12},{12... | collective-permute-start | bytes 589832 | tf_op jit(solution)/shard_map/ppermute | solution.py:36
  62.3 139.8 %copy-start.2 = (f32[256,2]{0,1:T(2,128)S(1)}, f32[256,2]{0,1:T(2,128)}, u32[]{:S(2)}) copy-start(f32[256,2]{0,1:T(2,128)} %param.8) | copy-start | bytes 6148
  62.3 166.5 %all-gather.5.cloned.1.call-start = ((), (), s32[]{:S(2)}) async-start(), calls=%async_computation.5 | async-start | bytes 1310720 | tf_op jit(solution)/shard_map/all_gather | solution.py:47
  65.5 192.2 %all-gather.9.cloned.1.call-start = ((), (), s32[]{:S(2)}) async-start(), calls=%async_computation.9 | async-start | bytes 1310720 | tf_op jit(solution)/shard_map/all_gather | solution.py:47
  111.1 175.6 %all-gather.7.cloned.1.call-start = ((), (), s32[]{:S(2)}) async-start(), calls=%async_computation.7 | async-start | bytes 1310720 | tf_op jit(solution)/shard_map/all_gather | solution.py:47
  156.7 159.1 %all-gather.11.cloned.1.call-start = ((), (), s32[]{:S(2)}) async-start(), calls=%async_computation.11 | async-start | bytes 1310720 | tf_op jit(solution)/shard_map/all_gather | solution.py:47
  232.9 101.4 %collective-permute-start = (bf16[128,768]{1,0:T(8,128)(2,1)S(1)}, bf16[128,768]{1,0:T(8,128)(2,1)S(1)}, u32[]{:S(2)}, u32[]{:S(2)}) collective-permute-start(bf16[128,768]{1,0:T(8,128)(2,1)S(1)} %fusion.56), channel_id=1, source_target_pairs={{0,1},{1,0},{2,3},{3,2},{4,5},{5,4},{6,7},{7,6},{8,9},{9,8},{10,11... | collective-permute-start | bytes 589832 | tf_op jit(solution)/shard_map/ppermute | solution.py:50
  261.8 59.6 %collective-permute-start.5 = (bf16[128,768]{1,0:T(8,128)(2,1)S(1)}, bf16[128,768]{1,0:T(8,128)(2,1)S(1)}, u32[]{:S(2)}, u32[]{:S(2)}) collective-permute-start(bf16[128,768]{1,0:T(8,128)(2,1)S(1)} %fusion.62), channel_id=1, source_target_pairs={{0,1},{1,0},{2,3},{3,2},{4,5},{5,4},{6,7},{7,6},{8,9},{9,8},{10,11... | collective-permute-start | bytes 589832 | tf_op jit(solution)/shard_map/ppermute | solution.py:50
  290.8 32.2 %collective-permute-start.2 = (bf16[128,768]{1,0:T(8,128)(2,1)S(1)}, bf16[128,768]{1,0:T(8,128)(2,1)S(1)}, u32[]{:S(2)}, u32[]{:S(2)}) collective-permute-start(bf16[128,768]{1,0:T(8,128)(2,1)S(1)} %fusion.59), channel_id=1, source_target_pairs={{0,1},{1,0},{2,3},{3,2},{4,5},{5,4},{6,7},{7,6},{8,9},{9,8},{10,11... | collective-permute-start | bytes 589832 | tf_op jit(solution)/shard_map/ppermute | solution.py:50
  319.9 6.6 %collective-permute-start.8 = (bf16[128,768]{1,0:T(8,128)(2,1)S(1)}, bf16[128,768]{1,0:T(8,128)(2,1)S(1)}, u32[]{:S(2)}, u32[]{:S(2)}) collective-permute-start(bf16[128,768]{1,0:T(8,128)(2,1)S(1)} %fusion.65), channel_id=1, source_target_pairs={{0,1},{1,0},{2,3},{3,2},{4,5},{5,4},{6,7},{7,6},{8,9},{9,8},{10,11... | collective-permute-start | bytes 589832 | tf_op jit(solution)/shard_map/ppermute | solution.py:50
  321.5 6.3 %collective-permute-start.6 = (bf16[128,768]{1,0:T(8,128)(2,1)S(1)}, bf16[128,768]{1,0:T(8,128)(2,1)S(1)}, u32[]{:S(2)}, u32[]{:S(2)}) collective-permute-start(bf16[128,768]{1,0:T(8,128)(2,1)S(1)} %add_convert_fusion.1), channel_id=1, source_target_pairs={{0,4},{2,6},{4,0},{6,2},{1,5},{3,7},{5,1},{7,3},{8,12},{10,14},{12... | collective-permute-start | bytes 589832 | tf_op jit(solution)/shard_map/ppermute | solution.py:55
  323.0 5.3 %collective-permute-start.3 = (bf16[128,768]{1,0:T(8,128)(2,1)S(1)}, bf16[128,768]{1,0:T(8,128)(2,1)S(1)}, u32[]{:S(2)}, u32[]{:S(2)}) collective-permute-start(bf16[128,768]{1,0:T(8,128)(2,1)S(1)} %add_convert_fusion.2), channel_id=1, source_target_pairs={{0,2},{2,0},{4,6},{6,4},{1,3},{3,1},{5,7},{7,5},{8,10},{10,8},{12,... | collective-permute-start | bytes 589832 | tf_op jit(solution)/shard_map/ppermute | solution.py:55
  326.5 7.2 %collective-permute-start.9 = (bf16[128,768]{1,0:T(8,128)(2,1)S(1)}, bf16[128,768]{1,0:T(8,128)(2,1)S(1)}, u32[]{:S(2)}, u32[]{:S(2)}) collective-permute-start(bf16[128,768]{1,0:T(8,128)(2,1)S(1)} %add_convert_fusion), channel_id=1, source_target_pairs={{0,6},{2,4},{4,2},{6,0},{1,7},{3,5},{5,3},{7,1},{8,14},{10,12},{12... | collective-permute-start | bytes 589832 | tf_op jit(solution)/shard_map/ppermute | solution.py:55
Sparse Core Ops, SparseCore 0:
  16.9 46.5 reduce-scatter.4
  65.9 43.1 reduce-scatter.8
  111.4 43.1 reduce-scatter.6
  156.9 43.1 reduce-scatter.10
  201.5 27.2 all-gather.4
  230.2 27.4 all-gather.8
  259.3 27.4 all-gather.6
  288.3 27.4 all-gather.10
